TPU v7x, 128 devices: a whole 4x4x4 slice. The times are simulated.
128 devices in a mesh: rep: 4 (over y_lo, core), fsdp: 32 (over y_hi, x, z).
Axes of the slice: x: 4, y: 4 (y_hi: 2, y_lo: 2; y = y_hi * 2 + y_lo), z: 4, core: 2. Of those that a mesh axis runs over, the one named last changes fastest.
Arguments:
- tokens: bfloat16 [2, 128, 128, 1024], P(None, ('rep', 'fsdp')), may hold values from -6 to 6
- segments: int32 [2, 128, 128], P(None, ('rep', 'fsdp')), may hold values from 0 to 31, never falling along the last dimension, each value on 1 to 64 neighbouring positions
- routes: int32 [2, 128, 128, 8], P(None, ('rep', 'fsdp')), may hold values from 0 to 31, all different within a row; in each aligned block of 128 rows (0 to 127, 128 to 255, ..., all dimensions but the last counted through in order) at most 48 rows name the same one
- cotangent: bfloat16 [2, 128, 128, 1024], P(None, ('rep', 'fsdp')), may hold values from -6 to 6
- attn_gain: bfloat16 [1024], P('fsdp'), may hold values from 0.5 to 1.5
- moe_gain: bfloat16 [1024], P('fsdp'), may hold values from 0.5 to 1.5
- w_query: bfloat16 [1024, 1024], P('fsdp'), may hold values from -0.75 to 0.75
- w_key: bfloat16 [1024, 512], P('fsdp'), may hold values from -0.75 to 0.75
- w_value: bfloat16 [1024, 512], P('fsdp'), may hold values from -0.1875 to 0.1875
- w_output: bfloat16 [1024, 1024], P('fsdp'), may hold values from -1.5 to 1.5
- w_router: bfloat16 [1024, 32], P('fsdp'), may hold values from -0.09375 to 0.09375
- w_gate: bfloat16 [32, 1024, 512], P('fsdp'), may hold values from -0.1875 to 0.1875
- w_up: bfloat16 [32, 1024, 512], P('fsdp'), may hold values from -0.1875 to 0.1875
- w_down: bfloat16 [32, 512, 1024], P('fsdp'), may hold values from -6 to 6
Outputs:
- output: bfloat16 [2, 128, 128, 1024], P(None, ('rep', 'fsdp'))
- grad_tokens: float32 [2, 128, 128, 1024], P(None, ('rep', 'fsdp'))
- grad_attn_gain: float32 [1024], P('fsdp')
- grad_moe_gain: float32 [1024], P('fsdp')
- grad_query: float32 [1024, 1024], P('fsdp')
- grad_key: float32 [1024, 512], P('fsdp')
- grad_value: float32 [1024, 512], P('fsdp')
- grad_w_output: float32 [1024, 1024], P('fsdp')
- grad_router: float32 [1024, 32], P('fsdp')
- grad_gate: float32 [32, 1024, 512], P('fsdp')
- grad_up: float32 [32, 1024, 512], P('fsdp')
- grad_down: float32 [32, 512, 1024], P('fsdp')
Inputs may be any that keep to these rules, and one draw needn't show every extreme that they name: `segments`: within a sequence segment numbers never fall; every segment has 1 to 64 tokens and some segment has exactly 64. `routes`: A token's 8 experts differ. Within one sequence no expert is named by more than 48 tokens, and in every draw some sequence names some expert exactly 48 times.
All inputs are finite; a program needn't handle non-finite values.
Results may differ from a plain program's by a relative error of at most 0.018.
Values may be sent and summed in bfloat16 or wider, within the bound.
A program may use at most 192 MiB of HBM per device.

v0:
```python
import math
import jax
import jax.numpy as jnp
from jax import lax
from jax.sharding import PartitionSpec as P

D = 1024
HEADS = 16
KV_HEADS = 8
HEAD_DIM = 64
EXPERTS = 32
TOPK = 8
CAP = 48
EPS = 1e-06
RESIDUAL = 0.22
ATT_SCALE = 0.015625
ROPE_BASE = 10000.0
NEG = -1000000000.0


def phases(segment):
    length = segment.shape[0]
    places = jnp.arange(length, dtype=jnp.int32)
    starts = jnp.concatenate([jnp.ones((1,), dtype=bool), segment[1:] != segment[:-1]])
    opening = lax.cummax(jnp.where(starts, places, 0), axis=0)
    offset = (places - opening).astype(jnp.float32)
    halves = HEAD_DIM // 2
    frequency = jnp.exp(
        -math.log(ROPE_BASE) * 2.0 * jnp.arange(halves).astype(jnp.float32) / HEAD_DIM
    )
    angles = offset[:, None] * frequency[None, :]
    angles = jnp.concatenate([angles, angles], axis=1)[:, None, :]
    visible = (places[None, :] <= places[:, None]) & (segment[:, None] == segment[None, :])
    return (jnp.cos(angles), jnp.sin(angles), visible)


def rotate(values, cos_table, sin_table):
    height = values.shape[0]
    per_head = values.reshape(height, -1, HEAD_DIM)
    halves = HEAD_DIM // 2
    turned = jnp.concatenate([-per_head[..., halves:], per_head[..., :halves]], axis=-1)
    return (per_head * cos_table + turned * sin_table).reshape(height, -1)


def slot_index(route_ids):
    flat_routes = route_ids.reshape(-1)
    choose = (flat_routes[:, None] == jnp.arange(EXPERTS, dtype=jnp.int32)[None, :]).astype(
        jnp.int32
    )
    before = jnp.cumsum(choose, axis=0) - choose
    slots = jnp.sum(before * choose, axis=1)
    return flat_routes * CAP + slots


def normalize(values, gain):
    scale = lax.rsqrt(jnp.mean(values * values, axis=-1, keepdims=True) + EPS)
    normed = values * scale
    return (normed, scale, normed * gain)


def normalize_back(grad_out, normed, scale, gain):
    grad_norm = grad_out * gain
    grad_in = scale * (grad_norm - normed * jnp.mean(grad_norm * normed, axis=-1, keepdims=True))
    return (grad_in, jnp.sum(grad_out * normed, axis=0))


def scores_of(query_low, key_low, visible):
    height = query_low.shape[0]
    query_four = query_low.reshape(height, KV_HEADS, HEADS // KV_HEADS, HEAD_DIM)
    key_three = key_low.reshape(height, KV_HEADS, HEAD_DIM)
    scores = (
        jnp.einsum("qkgd,skd->kgqs", query_four, key_three, preferred_element_type=jnp.float32)
        * ATT_SCALE
    )
    return jnp.where(visible[None, None], scores, NEG)


def attend(query_low, key_low, value_low, visible):
    height = query_low.shape[0]
    scores = scores_of(query_low, key_low, visible)
    highest = jnp.max(scores, axis=-1, keepdims=True)
    log_total = highest + jnp.log(jnp.sum(jnp.exp(scores - highest), axis=-1, keepdims=True))
    attention = jnp.exp(scores - log_total).astype(jnp.bfloat16)
    value_three = value_low.reshape(height, KV_HEADS, HEAD_DIM)
    attended = jnp.einsum(
        "kgqs,skd->qkgd", attention, value_three, preferred_element_type=jnp.float32
    )
    return (attended.reshape(height, -1).astype(jnp.bfloat16), log_total)


def attend_back(query_low, key_low, value_low, visible, log_total, grad_mixed):
    height = query_low.shape[0]
    query_four = query_low.reshape(height, KV_HEADS, HEADS // KV_HEADS, HEAD_DIM)
    key_three = key_low.reshape(height, KV_HEADS, HEAD_DIM)
    value_three = value_low.reshape(height, KV_HEADS, HEAD_DIM)
    attention = jnp.exp(scores_of(query_low, key_low, visible) - log_total)
    attention_low = attention.astype(jnp.bfloat16)
    grad_four = grad_mixed.reshape(height, KV_HEADS, HEADS // KV_HEADS, HEAD_DIM)
    value_grad = jnp.einsum(
        "kgqs,qkgd->skd", attention_low, grad_four, preferred_element_type=jnp.float32
    )
    prob_grad = jnp.einsum(
        "qkgd,skd->kgqs", grad_four, value_three, preferred_element_type=jnp.float32
    )
    inner_prod = jnp.sum(attention * prob_grad, axis=-1, keepdims=True)
    score_grad = (attention * (prob_grad - inner_prod)).astype(jnp.bfloat16)
    query_grad = (
        jnp.einsum("kgqs,skd->qkgd", score_grad, key_three, preferred_element_type=jnp.float32)
        * ATT_SCALE
    )
    key_grad = (
        jnp.einsum("kgqs,qkgd->skd", score_grad, query_four, preferred_element_type=jnp.float32)
        * ATT_SCALE
    )
    return (
        query_grad.reshape(height, -1),
        key_grad.reshape(height, -1),
        value_grad.reshape(height, -1),
    )


def fetch_dense(attn_gain, moe_gain, w_query, w_key, w_value, w_output, w_router):
    return (
        lax.all_gather(attn_gain, "fsdp", axis=0, tiled=True),
        lax.all_gather(moe_gain, "fsdp", axis=0, tiled=True),
        lax.all_gather(w_query, "fsdp", axis=0, tiled=True),
        lax.all_gather(w_key, "fsdp", axis=0, tiled=True),
        lax.all_gather(w_value, "fsdp", axis=0, tiled=True),
        lax.all_gather(w_output, "fsdp", axis=0, tiled=True),
        lax.all_gather(w_router, "fsdp", axis=0, tiled=True),
    )


def reduce_dense(grads):
    return (
        lax.psum_scatter(grads[0], "fsdp", scatter_dimension=0, tiled=True),
        lax.psum_scatter(grads[1], "fsdp", scatter_dimension=0, tiled=True),
        lax.psum_scatter(grads[2], "fsdp", scatter_dimension=0, tiled=True),
        lax.psum_scatter(grads[3], "fsdp", scatter_dimension=0, tiled=True),
        lax.psum_scatter(grads[4], "fsdp", scatter_dimension=0, tiled=True),
        lax.psum_scatter(grads[5], "fsdp", scatter_dimension=0, tiled=True),
        lax.psum_scatter(grads[6], "fsdp", scatter_dimension=0, tiled=True),
    )


def combine_sum(current, update):
    return current + update


def on_device(
    tokens,
    segments,
    routes,
    cotangent,
    attn_gain,
    moe_gain,
    w_query,
    w_key,
    w_value,
    w_output,
    w_router,
    w_gate,
    w_up,
    w_down,
):
    micro = tokens.shape[0]
    length = tokens.shape[2]
    groups = lax.axis_size("fsdp")
    local_experts = w_gate.shape[0]
    shards = (attn_gain, moe_gain, w_query, w_key, w_value, w_output, w_router)
    totals = tuple((jnp.zeros(member.shape, jnp.float32) for member in shards))
    grad_gate = jnp.zeros(w_gate.shape, jnp.float32)
    grad_up = jnp.zeros(w_up.shape, jnp.float32)
    grad_down = jnp.zeros(w_down.shape, jnp.float32)
    outputs = []
    grads_in = []
    expert_ids = jnp.arange(EXPERTS, dtype=jnp.int32)
    for number in range(micro):
        dense_set = fetch_dense(attn_gain, moe_gain, w_query, w_key, w_value, w_output, w_router)
        gain_one = dense_set[0].astype(jnp.float32)
        gain_two = dense_set[1].astype(jnp.float32)
        inputs = tokens[number, 0].astype(jnp.float32)
        segment = segments[number, 0]
        route_ids = routes[number, 0]
        cos_table, sin_table, visible = phases(segment)
        normed_one, scale_one, hidden_one = normalize(inputs, gain_one)
        hidden_low = hidden_one.astype(jnp.bfloat16)
        query_raw = jnp.dot(hidden_low, dense_set[2], preferred_element_type=jnp.float32)
        key_raw = jnp.dot(hidden_low, dense_set[3], preferred_element_type=jnp.float32)
        value_low = jnp.dot(hidden_low, dense_set[4], preferred_element_type=jnp.float32).astype(
            jnp.bfloat16
        )
        query_low = rotate(query_raw, cos_table, sin_table).astype(jnp.bfloat16)
        key_low = rotate(key_raw, cos_table, sin_table).astype(jnp.bfloat16)
        mixed_low, log_total = attend(query_low, key_low, value_low, visible)
        branch = jnp.dot(mixed_low, dense_set[5], preferred_element_type=jnp.float32)
        middle = inputs + RESIDUAL * branch
        normed_two, scale_two, hidden_two = normalize(middle, gain_two)
        routed_low = hidden_two.astype(jnp.bfloat16)
        logits = jnp.dot(routed_low, dense_set[6], preferred_element_type=jnp.float32)
        choose = (route_ids[:, :, None] == expert_ids[None, None, :]).astype(jnp.float32)
        chosen = jnp.einsum("tke,te->tk", choose, logits)
        gate_weights = jax.nn.softmax(chosen, axis=-1)
        places = slot_index(route_ids)
        copies = jnp.repeat(routed_low, TOPK, axis=0)
        outgoing = (
            jnp.zeros((EXPERTS * CAP, D), jnp.bfloat16)
            .at[places]
            .set(copies)
            .reshape(EXPERTS, CAP, D)
        )
        arrived = lax.all_to_all(outgoing, "fsdp", split_axis=0, concat_axis=0, tiled=True).reshape(
            groups, local_experts, CAP, D
        )
        gate_act = jnp.einsum("secd,edf->secf", arrived, w_gate, preferred_element_type=jnp.float32)
        up_act = jnp.einsum("secd,edf->secf", arrived, w_up, preferred_element_type=jnp.float32)
        sigmoid_act = jax.nn.sigmoid(gate_act)
        swish_act = gate_act * sigmoid_act
        inner_low = (swish_act * up_act).astype(jnp.bfloat16)
        expert_out = jnp.einsum(
            "secf,efd->secd", inner_low, w_down, preferred_element_type=jnp.float32
        ).astype(jnp.bfloat16)
        returned = lax.all_to_all(
            expert_out.reshape(groups * local_experts, CAP, D),
            "fsdp",
            split_axis=0,
            concat_axis=0,
            tiled=True,
        ).reshape(EXPERTS * CAP, D)
        picked = returned[places].reshape(length, TOPK, D)
        mixture = jnp.sum(gate_weights[:, :, None] * picked, axis=1)
        result = middle + RESIDUAL * mixture
        outputs.append(result.astype(jnp.bfloat16))
        dense_set = fetch_dense(attn_gain, moe_gain, w_query, w_key, w_value, w_output, w_router)
        upstream = cotangent[number, 0].astype(jnp.float32)
        grad_mix = RESIDUAL * upstream
        gate_grad = jnp.sum(picked * grad_mix[:, None, :], axis=-1)
        slot_grad = (
            (gate_weights[:, :, None] * grad_mix[:, None, :])
            .astype(jnp.bfloat16)
            .reshape(length * TOPK, D)
        )
        sending = (
            jnp.zeros((EXPERTS * CAP, D), jnp.bfloat16)
            .at[places]
            .set(slot_grad)
            .reshape(EXPERTS, CAP, D)
        )
        arrived_grad = lax.all_to_all(
            sending, "fsdp", split_axis=0, concat_axis=0, tiled=True
        ).reshape(groups, local_experts, CAP, D)
        inner_grad = jnp.einsum(
            "secd,efd->secf", arrived_grad, w_down, preferred_element_type=jnp.float32
        )
        grad_down = grad_down + jnp.einsum(
            "secf,secd->efd", inner_low, arrived_grad, preferred_element_type=jnp.float32
        )
        gate_pre = (
            inner_grad * up_act * sigmoid_act * (1.0 + gate_act * (1.0 - sigmoid_act))
        ).astype(jnp.bfloat16)
        up_pre = (inner_grad * swish_act).astype(jnp.bfloat16)
        grad_gate = grad_gate + jnp.einsum(
            "secd,secf->edf", arrived, gate_pre, preferred_element_type=jnp.float32
        )
        grad_up = grad_up + jnp.einsum(
            "secd,secf->edf", arrived, up_pre, preferred_element_type=jnp.float32
        )
        feature_grad = jnp.einsum(
            "secf,edf->secd", gate_pre, w_gate, preferred_element_type=jnp.float32
        )
        feature_grad = feature_grad + jnp.einsum(
            "secf,edf->secd", up_pre, w_up, preferred_element_type=jnp.float32
        )
        back_rows = lax.all_to_all(
            feature_grad.astype(jnp.bfloat16).reshape(groups * local_experts, CAP, D),
            "fsdp",
            split_axis=0,
            concat_axis=0,
            tiled=True,
        ).reshape(EXPERTS * CAP, D)
        routed_grad = jnp.sum(
            back_rows[places].reshape(length, TOPK, D).astype(jnp.float32), axis=1
        )
        choice_grad = gate_weights * (
            gate_grad - jnp.sum(gate_weights * gate_grad, axis=-1, keepdims=True)
        )
        logit_grad = jnp.einsum("tke,tk->te", choose, choice_grad).astype(jnp.bfloat16)
        router_grad = jnp.einsum(
            "td,te->de", routed_low, logit_grad, preferred_element_type=jnp.float32
        )
        routed_grad = routed_grad + jnp.einsum(
            "te,de->td", logit_grad, dense_set[6], preferred_element_type=jnp.float32
        )
        middle_grad, gain_two_grad = normalize_back(routed_grad, normed_two, scale_two, gain_two)
        middle_grad = middle_grad + upstream
        branch_low = (RESIDUAL * middle_grad).astype(jnp.bfloat16)
        output_grad = jnp.einsum(
            "tf,td->fd", mixed_low, branch_low, preferred_element_type=jnp.float32
        )
        mixed_grad = jnp.einsum(
            "td,fd->tf", branch_low, dense_set[5], preferred_element_type=jnp.float32
        ).astype(jnp.bfloat16)
        query_grad, key_grad, value_grad = attend_back(
            query_low, key_low, value_low, visible, log_total, mixed_grad
        )
        query_low_grad = rotate(query_grad, cos_table, -sin_table).astype(jnp.bfloat16)
        key_low_grad = rotate(key_grad, cos_table, -sin_table).astype(jnp.bfloat16)
        value_low_grad = value_grad.astype(jnp.bfloat16)
        wq_grad = jnp.einsum(
            "td,tf->df", hidden_low, query_low_grad, preferred_element_type=jnp.float32
        )
        wk_grad = jnp.einsum(
            "td,tf->df", hidden_low, key_low_grad, preferred_element_type=jnp.float32
        )
        wv_grad = jnp.einsum(
            "td,tf->df", hidden_low, value_low_grad, preferred_element_type=jnp.float32
        )
        hidden_grad = jnp.einsum(
            "tf,df->td", query_low_grad, dense_set[2], preferred_element_type=jnp.float32
        )
        hidden_grad = hidden_grad + jnp.einsum(
            "tf,df->td", key_low_grad, dense_set[3], preferred_element_type=jnp.float32
        )
        hidden_grad = hidden_grad + jnp.einsum(
            "tf,df->td", value_low_grad, dense_set[4], preferred_element_type=jnp.float32
        )
        normed_grad, gain_one_grad = normalize_back(hidden_grad, normed_one, scale_one, gain_one)
        grads_in.append(middle_grad + normed_grad)
        dense_grads = (
            gain_one_grad,
            gain_two_grad,
            wq_grad,
            wk_grad,
            wv_grad,
            output_grad,
            router_grad,
        )
        reduced = reduce_dense(dense_grads)
        totals = tuple((combine_sum(current, update) for current, update in zip(totals, reduced)))
    summed = lax.psum(
        (
            totals[0],
            totals[1],
            totals[2],
            totals[3],
            totals[4],
            totals[5],
            totals[6],
            grad_gate,
            grad_up,
            grad_down,
        ),
        "rep",
    )
    return (
        jnp.stack(outputs)[:, None],
        jnp.stack(grads_in)[:, None],
        summed[0],
        summed[1],
        summed[2],
        summed[3],
        summed[4],
        summed[5],
        summed[6],
        summed[7],
        summed[8],
        summed[9],
    )


def solution(mesh):
    placed = (
        P(None, ("rep", "fsdp"), None, None),
        P(None, ("rep", "fsdp"), None),
        P(None, ("rep", "fsdp"), None, None),
        P(None, ("rep", "fsdp"), None, None),
        P("fsdp"),
        P("fsdp"),
        P("fsdp", None),
        P("fsdp", None),
        P("fsdp", None),
        P("fsdp", None),
        P("fsdp", None),
        P("fsdp", None, None),
        P("fsdp", None, None),
        P("fsdp", None, None),
    )
    return jax.shard_map(
        on_device,
        mesh=mesh,
        in_specs=placed,
        out_specs=(
            P(None, ("rep", "fsdp"), None, None),
            P(None, ("rep", "fsdp"), None, None),
            P("fsdp"),
            P("fsdp"),
            P("fsdp", None),
            P("fsdp", None),
            P("fsdp", None),
            P("fsdp", None),
            P("fsdp", None),
            P("fsdp", None, None),
            P("fsdp", None, None),
            P("fsdp", None, None),
        ),
        check_vma=False,
    )
```

profile of v0, /device:TPU:1, one launch (start us, length us, event | category | flops | bytes accessed | tf_op | source)
XLA Modules:
  0.0 1932.4 jit_solution(3319828074950691068)
XLA Ops:
  16.1 84.6 %all-reduce.7 = (bf16[1024]{0:T(1024)(128)(2,1)S(1)}, bf16[1024]{0:T(1024)(128)(2,1)S(1)}) all-reduce(bf16[1024]{0:T(1024)(128)(2,1)S(1)} %dynamic-update-slice, bf16[1024]{0:T(1024)(128)(2,1)S(1)} %dynamic-update-slice.1), channel_id=1, replica_groups=mesh['rep'=4,'fsdp'=32] {'fsdp'}, use_global_device_ids=true, to_apply=%add | all-reduce | flops 2048 | bytes 8192
  117.0 28.5 %all-gather.7.cloned.1.call-done = bf16[1024,512]{1,0:T(8,128)(2,1)} async-done(((bf16[32,512]{1,0:T(8,128)(2,1)}), bf16[1024,512]{1,0:T(8,128)(2,1)}) %all-gather.7.cloned.1.call-update) | async-done | bytes 1048592 | tf_op jit(solution)/shard_map/all_gather | solution.py:127
  147.6 69.3 %all-gather.9.cloned.1.call-done = bf16[1024,1024]{1,0:T(8,128)(2,1)} async-done(((bf16[32,1024]{1,0:T(8,128)(2,1)}), bf16[1024,1024]{1,0:T(8,128)(2,1)}) %all-gather.9.cloned.1.call-update) | async-done | bytes 2097168 | tf_op jit(solution)/shard_map/all_gather | solution.py:126
  225.7 61.9 %all-gather.11.cloned.1.call-done = bf16[1024,1024]{1,0:T(8,128)(2,1)} async-done(((bf16[32,1024]{1,0:T(8,128)(2,1)}), bf16[1024,1024]{1,0:T(8,128)(2,1)}) %all-gather.11.cloned.1.call-update) | async-done | bytes 2097168 | tf_op jit(solution)/shard_map/all_gather | solution.py:129
  303.7 107.3 %all_gather.20 = bf16[1024,32]{1,0:T(8,128)(2,1)S(1)} all-gather(bf16[32,32]{1,0:T(8,128)(2,1)S(1)} %copy-done.108), channel_id=1, replica_groups=mesh['rep'=4,'fsdp'=32] {'fsdp'}, dimensions={0}, use_global_device_ids=true | all-gather | bytes 67584 | tf_op jit(solution)/shard_map/all_gather | solution.py:130
  437.6 23.1 %all-to-all-done.4 = bf16[32,48,1024]{2,1,0:T(8,128)(2,1)} async-done(((bf16[32,48,1024]{2,1,0:T(8,128)(2,1)}), bf16[32,48,1024]{2,1,0:T(8,128)(2,1)}, u32[]{:S(2)}, u32[]{:S(2)}) %all-to-all-start.4) | async-done | bytes 3145760 | tf_op jit(solution)/shard_map/all_to_all | solution.py:249
  476.0 13.0 all-to-all-start.1
  510.8 13.0 all-to-all-done.1
  523.8 22.2 %all-to-all-start.5 = ((bf16[32,48,1024]{2,1,0:T(8,128)(2,1)}), bf16[32,48,1024]{2,1,0:T(8,128)(2,1)}, u32[]{:S(2)}, u32[]{:S(2)}) async-start(bf16[32,48,1024]{2,1,0:T(8,128)(2,1)} %add_convert_fusion.1), calls=%async_computation.5 | async-start | bytes 6291456 | tf_op jit(solution)/shard_map/all_to_all | solution.py:274
  563.9 18.4 all-to-all-done.5
  601.8 13.1 all-to-all-start.2
  624.4 30.1 %all-to-all-done.2 = bf16[32,48,1024]{2,1,0:T(8,128)(2,1)} async-done(((bf16[32,48,1024]{2,1,0:T(8,128)(2,1)}), bf16[32,48,1024]{2,1,0:T(8,128)(2,1)}, u32[]{:S(2)}, u32[]{:S(2)}) %all-to-all-start.2) | async-done | bytes 3145760 | tf_op jit(solution)/shard_map/all_to_all | solution.py:212
  670.5 34.6 %all-to-all-done.6 = bf16[32,48,1024]{2,1,0:T(8,128)(2,1)} async-done(((bf16[32,48,1024]{2,1,0:T(8,128)(2,1)}), bf16[32,48,1024]{2,1,0:T(8,128)(2,1)}, u32[]{:S(2)}, u32[]{:S(2)}) %all-to-all-start.6) | async-done | bytes 3145760 | tf_op jit(solution)/shard_map/all_to_all | solution.py:249
  737.3 33.3 %all-to-all-done.3 = bf16[32,48,1024]{2,1,0:T(8,128)(2,1)} async-done(((bf16[32,48,1024]{2,1,0:T(8,128)(2,1)}), bf16[32,48,1024]{2,1,0:T(8,128)(2,1)}, u32[]{:S(2)}, u32[]{:S(2)}) %all-to-all-start.3) | async-done | bytes 3145760 | tf_op jit(solution)/shard_map/all_to_all | solution.py:223
  770.7 10.6 all-to-all-start.7
  795.2 27.0 %all-to-all-done.7 = bf16[32,48,1024]{2,1,0:T(8,128)(2,1)S(1)} async-done(((bf16[32,48,1024]{2,1,0:T(8,128)(2,1)}), bf16[32,48,1024]{2,1,0:T(8,128)(2,1)S(1)}, u32[]{:S(2)}, u32[]{:S(2)}) %all-to-all-start.7) | async-done | bytes 3145760 | tf_op jit(solution)/shard_map/all_to_all | solution.py:274
  895.4 114.7 %reduce-scatter.10.cloned.1.call-done = f32[32,512]{1,0:T(8,128)} async-done(((f32[1024,512]{1,0:T(8,128)}), f32[32,512]{1,0:T(8,128)}) %reduce-scatter.10.cloned.1.call-update) | async-done | bytes 65552 | tf_op jit(solution)/shard_map/reduce_scatter | solution.py:140
  1010.2 184.8 %reduce-scatter.8.cloned.1.call-done = f32[32,512]{1,0:T(8,128)} async-done(((f32[1024,512]{1,0:T(8,128)}), f32[32,512]{1,0:T(8,128)}) %reduce-scatter.8.cloned.1.call-update) | async-done | bytes 65552 | tf_op jit(solution)/shard_map/reduce_scatter | solution.py:139
  1195.0 191.4 %reduce-scatter.12.cloned.1.call-done = f32[32,1024]{1,0:T(8,128)} async-done(((f32[1024,1024]{1,0:T(8,128)}), f32[32,1024]{1,0:T(8,128)}) %reduce-scatter.12.cloned.1.call-update) | async-done | bytes 131088 | tf_op jit(solution)/shard_map/reduce_scatter | solution.py:141
  1386.4 189.5 %reduce-scatter.6.cloned.1.call-done = f32[32,1024]{1,0:T(8,128)} async-done(((f32[1024,1024]{1,0:T(8,128)}), f32[32,1024]{1,0:T(8,128)}) %reduce-scatter.6.cloned.1.call-update) | async-done | bytes 131088 | tf_op jit(solution)/shard_map/reduce_scatter | solution.py:138
  1584.7 77.8 %all-reduce.4 = (f32[1024]{0:T(1024)S(1)}, f32[1024]{0:T(1024)S(1)}) all-reduce(f32[1024]{0:T(1024)S(1)} %add.332, f32[1024]{0:T(1024)S(1)} %copy-done.96), channel_id=9, replica_groups=mesh['rep'=4,'fsdp'=32] {'fsdp'}, use_global_device_ids=true, to_apply=%region_39.40.clone | all-reduce | flops 2048 | bytes 16384
  1665.9 89.4 %reduce-scatter.14.cloned.1.call-done = f32[32,32]{1,0:T(8,128)} async-done(((f32[1024,32]{1,0:T(8,128)}), f32[32,32]{1,0:T(8,128)}) %reduce-scatter.14.cloned.1.call-update) | async-done | bytes 4112 | tf_op jit(solution)/shard_map/reduce_scatter | solution.py:142
  1755.2 36.6 %all-reduce.5 = (f32[32]{0:T(128)}, f32[32]{0:T(128)}, f32[32,32]{1,0:T(8,128)}) all-reduce(f32[32]{0:T(128)S(1)} %dynamic-slice.3, f32[32]{0:T(128)S(1)} %dynamic-slice.5, f32[32,32]{1,0:T(8,128)} %reduce-scatter.14.cloned.1.call-done), channel_id=1, replica_groups=mesh['rep'=4,'fsdp'=32] {'rep'}, use_global_device_ids=true, to_apply=%region_42.43 | all-reduce | flops 1088 | bytes 8704 | tf_op jit(solution)/shard_map/psum | solution.py:340
  1791.8 120.3 %all-reduce.10.cloned.1.call-done = (f32[32,1024]{1,0:T(8,128)}, f32[32,512]{1,0:T(8,128)}, f32[32,512]{1,0:T(8,128)}, f32[32,1024]{1,0:T(8,128)}, f32[1,1024,51...) async-done(((f32[32,1024]{1,0:T(8,128)}, f32[32,512]{1,0:T(8,128)}, f32[32,512]{1,0:T(8,128)}, f32[32,1024]{1,0:T(8,128)}, f32[1,1024,512]{2,1,0:T(8,128)}, ...) | async-done | bytes 6684688 | tf_op jit(solution)/shard_map/psum | solution.py:340
  (477 shorter events, 319.8 us)
Async XLA Ops:
  7.2 457.7 %copy-start = (bf16[1,1024,512]{2,1,0:T(8,128)(2,1)S(1)}, bf16[1,1024,512]{2,1,0:T(8,128)(2,1)}, u32[]{:S(2)}) copy-start(bf16[1,1024,512]{2,1,0:T(8,128)(2,1)} %param.25) | copy-start | bytes 3145732
  7.2 106.8 %copy-start.103 = (s32[2,1,128]{2,1,0:T(1,128)S(1)}, s32[2,1,128]{2,1,0:T(1,128)}, u32[]{:S(2)}) copy-start(s32[2,1,128]{2,1,0:T(1,128)} %param.15) | copy-start | bytes 3076
  7.2 108.0 %copy-start.2 = (bf16[2,1,128,1024]{3,2,1,0:T(8,128)(2,1)S(1)}, bf16[2,1,128,1024]{3,2,1,0:T(8,128)(2,1)}, u32[]{:S(2)}) copy-start(bf16[2,1,128,1024]{3,2,1,0:T(8,128)(2,1)} %param.14) | copy-start | bytes 1572868
  7.2 108.0 %all-gather.5.cloned.1.call-start = ((), (), s32[]{:S(2)}) async-start(), calls=%async_computation.13 | async-start | bytes 1081344 | tf_op jit(solution)/shard_map/all_gather | solution.py:128
  8.0 137.5 %all-gather.7.cloned.1.call-start = ((), (), s32[]{:S(2)}) async-start(), calls=%async_computation.14 | async-start | bytes 1081344 | tf_op jit(solution)/shard_map/all_gather | solution.py:127
  8.7 208.1 %all-gather.9.cloned.1.call-start = ((), (), s32[]{:S(2)}) async-start(), calls=%async_computation.15 | async-start | bytes 2162688 | tf_op jit(solution)/shard_map/all_gather | solution.py:126
  9.4 278.1 %all-gather.11.cloned.1.call-start = ((), (), s32[]{:S(2)}) async-start(), calls=%async_computation.16 | async-start | bytes 2162688 | tf_op jit(solution)/shard_map/all_gather | solution.py:129
  103.2 120.0 %copy-start.68 = (f32[128,64]{0,1:T(8,128)}, f32[128,64]{0,1:T(8,128)S(1)}, u32[]{:S(2)}) copy-start(f32[128,64]{0,1:T(8,128)S(1)} %get-tuple-element.115) | copy-start | bytes 98308
  114.5 176.1 %copy-start.94 = (s32[1024,1]{0,1:T(1,128)}, s32[1024,1]{0,1:T(1,128)S(1)}, u32[]{:S(2)}) copy-start(s32[1024,1]{0,1:T(1,128)S(1)} %compare_select_fusion.1) | copy-start | bytes 12292
  116.9 107.6 %copy-start.50 = (bf16[128,512]{0,1:T(8,128)(2,1)}, bf16[128,512]{0,1:T(8,128)(2,1)S(1)}, u32[]{:S(2)}) copy-start(bf16[128,512]{0,1:T(8,128)(2,1)S(1)} %copy.80) | copy-start | bytes 393220
  298.0 128.3 %all-to-all-start = ((bf16[32,48,1024]{2,1,0:T(8,128)(2,1)}), bf16[32,48,1024]{2,1,0:T(8,128)(2,1)}, u32[]{:S(2)}, u32[]{:S(2)}) async-start(bf16[32,48,1024]{2,1,0:T(8,128)(2,1)} %bitcast.622), calls=%async_computation | async-start | bytes 6291456 | tf_op jit(solution)/shard_map/all_to_all | solution.py:212
  426.3 34.4 %all-to-all-start.4 = ((bf16[32,48,1024]{2,1,0:T(8,128)(2,1)}), bf16[32,48,1024]{2,1,0:T(8,128)(2,1)}, u32[]{:S(2)}, u32[]{:S(2)}) async-start(bf16[32,48,1024]{2,1,0:T(8,128)(2,1)} %bitcast.624), calls=%async_computation.4 | async-start | bytes 6291456 | tf_op jit(solution)/shard_map/all_to_all | solution.py:249
  476.0 47.8 %all-to-all-start.1 = ((bf16[32,48,1024]{2,1,0:T(8,128)(2,1)}), bf16[32,48,1024]{2,1,0:T(8,128)(2,1)}, u32[]{:S(2)}, u32[]{:S(2)}) async-start(bf16[32,48,1024]{2,1,0:T(8,128)(2,1)} %convolution_convert_fusion.1), calls=%async_computation.1 | async-start | bytes 6291456 | tf_op jit(solution)/shard_map/all_to_all | solution.py:223
  523.8 58.5 %all-to-all-start.5 = ((bf16[32,48,1024]{2,1,0:T(8,128)(2,1)}), bf16[32,48,1024]{2,1,0:T(8,128)(2,1)}, u32[]{:S(2)}, u32[]{:S(2)}) async-start(bf16[32,48,1024]{2,1,0:T(8,128)(2,1)} %add_convert_fusion.1), calls=%async_computation.5 | async-start | bytes 6291456 | tf_op jit(solution)/shard_map/all_to_all | solution.py:274
  601.8 52.7 %all-to-all-start.2 = ((bf16[32,48,1024]{2,1,0:T(8,128)(2,1)}), bf16[32,48,1024]{2,1,0:T(8,128)(2,1)}, u32[]{:S(2)}, u32[]{:S(2)}) async-start(bf16[32,48,1024]{2,1,0:T(8,128)(2,1)} %bitcast.623), calls=%async_computation.2 | async-start | bytes 6291456 | tf_op jit(solution)/shard_map/all_to_all | solution.py:212
  654.5 50.6 %all-to-all-start.6 = ((bf16[32,48,1024]{2,1,0:T(8,128)(2,1)}), bf16[32,48,1024]{2,1,0:T(8,128)(2,1)}, u32[]{:S(2)}, u32[]{:S(2)}) async-start(bf16[32,48,1024]{2,1,0:T(8,128)(2,1)} %bitcast.625), calls=%async_computation.6 | async-start | bytes 6291456 | tf_op jit(solution)/shard_map/all_to_all | solution.py:249
  720.0 50.7 %all-to-all-start.3 = ((bf16[32,48,1024]{2,1,0:T(8,128)(2,1)}), bf16[32,48,1024]{2,1,0:T(8,128)(2,1)}, u32[]{:S(2)}, u32[]{:S(2)}) async-start(bf16[32,48,1024]{2,1,0:T(8,128)(2,1)} %convolution_convert_fusion), calls=%async_computation.3 | async-start | bytes 6291456 | tf_op jit(solution)/shard_map/all_to_all | solution.py:223
  770.7 51.5 %all-to-all-start.7 = ((bf16[32,48,1024]{2,1,0:T(8,128)(2,1)}), bf16[32,48,1024]{2,1,0:T(8,128)(2,1)S(1)}, u32[]{:S(2)}, u32[]{:S(2)}) async-start(bf16[32,48,1024]{2,1,0:T(8,128)(2,1)} %add_convert_fusion), calls=%async_computation.7 | async-start | bytes 6291456 | tf_op jit(solution)/shard_map/all_to_all | solution.py:274
  781.3 228.8 %reduce-scatter.10.cloned.1.call-start = ((), (), s32[]{:S(2)}) async-start(), calls=%async_computation.19 | async-start | bytes 2162688 | tf_op jit(solution)/shard_map/reduce_scatter | solution.py:140
  846.1 348.9 %reduce-scatter.8.cloned.1.call-start = ((), (), s32[]{:S(2)}) async-start(), calls=%async_computation.18 | async-start | bytes 2162688 | tf_op jit(solution)/shard_map/reduce_scatter | solution.py:139
  852.7 533.7 %reduce-scatter.12.cloned.1.call-start = ((), (), s32[]{:S(2)}) async-start(), calls=%async_computation.20 | async-start | bytes 4325376 | tf_op jit(solution)/shard_map/reduce_scatter | solution.py:141
  856.5 719.4 %reduce-scatter.6.cloned.1.call-start = ((), (), s32[]{:S(2)}) async-start(), calls=%async_computation.17 | async-start | bytes 4325376 | tf_op jit(solution)/shard_map/reduce_scatter | solution.py:138
  863.9 891.3 %reduce-scatter.14.cloned.1.call-start = ((), (), s32[]{:S(2)}) async-start(), calls=%async_computation.21 | async-start | bytes 540672 | tf_op jit(solution)/shard_map/reduce_scatter | solution.py:142
  888.9 1023.2 %all-reduce.10.cloned.1.call-start = ((), (), s32[]{:S(2)}) async-start(), calls=%async_computation.22 | async-start | bytes 13369344 | tf_op jit(solution)/shard_map/psum | solution.py:340
  (118 other events, 1443.1 us)
Sparse Core Ops, SparseCore 0:
  11.0 67.9 all-gather.4
  82.0 63.4 all-gather.6
  148.6 68.2 all-gather.8
  219.8 67.6 all-gather.10
  846.2 163.9 reduce-scatter.9
  1013.1 181.8 reduce-scatter.7
  1197.3 188.9 reduce-scatter.11
  1388.8 187.0 reduce-scatter.5
  1578.2 176.9 reduce-scatter.13
  1759.0 153.0 all-reduce.9
where the time goes:
time: 1940 us; the launch traced here: 1930 us
  waiting for transfers between devices  1230 us (63%)
  blocking collectives  306 us (16%)
  matrix products  132 us (7%)
  starting transfers between devices  90.4 us (5%)
  local copies, waits for them, and re-layouts  81.1 us (4%)
  other arithmetic  72.8 us (4%)
    reduce_scatter x1, waiting for transfers between devices, reduce_dense(): lax.psum_scatter(grads[5], 'fsdp', scatter_dimension=0, tiled=True)  191 us
    reduce_scatter x1, waiting for transfers between devices, reduce_dense(): lax.psum_scatter(grads[2], 'fsdp', scatter_dimension=0, tiled=True)  189 us
    reduce_scatter x1, waiting for transfers between devices, reduce_dense(): lax.psum_scatter(grads[3], 'fsdp', scatter_dimension=0, tiled=True)  185 us
    unnamed x2, blocking collectives  162 us
    psum x1, waiting for transfers between devices, on_device(): lax.psum((totals[0], totals[1], totals[2], totals[3], totals[4], totals[5...  120 us
    reduce_scatter x1, waiting for transfers between devices, reduce_dense(): lax.psum_scatter(grads[4], 'fsdp', scatter_dimension=0, tiled=True)  115 us
    all_gather x1, blocking collectives, fetch_dense(): lax.all_gather(w_router, 'fsdp', axis=0, tiled=True)  107 us
    reduce_scatter x1, waiting for transfers between devices, reduce_dense(): lax.psum_scatter(grads[6], 'fsdp', scatter_dimension=0, tiled=True)  89.4 us
  transfers between devices with their start and end apart: 18, of which 16 were waited for; matrix products, arithmetic and copies ran while one was open for 9% of the time, Pallas kernels for 0%

commit v1 on v0

--- a/solution.py
+++ b/solution.py
@@ -127,7 +127,9 @@
         lax.all_gather(w_key, "fsdp", axis=0, tiled=True),
         lax.all_gather(w_value, "fsdp", axis=0, tiled=True),
         lax.all_gather(w_output, "fsdp", axis=0, tiled=True),
-        lax.all_gather(w_router, "fsdp", axis=0, tiled=True),
+        jnp.concatenate(
+            lax.all_to_all(jnp.stack([w_router] * lax.axis_size("fsdp")), "fsdp", 0, 0), axis=0
+        ),
     )
 
 

time: 1940 us -> 1880 us (0.969)
  blocking collectives: 306 us -> 197 us
  waiting for transfers between devices: 1230 us -> 1270 us
    all_gather x1 -> x0, blocking collectives: 107 us -> none  [fetch_dense(): lax.all_gather(w_router, 'fsdp', axis=0, tiled=True)]
    all_to_all x2, waiting for transfers between devices: 30.1 us -> 54.2 us  [on_device(): lax.all_to_all(outgoing, 'fsdp', split_axis=0, concat_axis=0, tiled=True)]
  transfers between devices with their start and end apart: 18 -> 19, of which waited for: 16 -> 17; matrix products, arithmetic and copies ran while one was open for 9% -> 10% of each run, Pallas kernels for 0% -> 0%
where the time goes in v1:
time: 1880 us; the launch traced here: 1870 us
  waiting for transfers between devices  1270 us (68%)
  blocking collectives  197 us (10%)
  matrix products  132 us (7%)
  starting transfers between devices  99.6 us (5%)
  local copies, waits for them, and re-layouts  82.8 us (4%)
  other arithmetic  71.8 us (4%)
    reduce_scatter x1, waiting for transfers between devices, reduce_dense(): lax.psum_scatter(grads[5], 'fsdp', scatter_dimension=0, tiled=True)  191 us
    reduce_scatter x1, waiting for transfers between devices, reduce_dense(): lax.psum_scatter(grads[2], 'fsdp', scatter_dimension=0, tiled=True)  190 us
    reduce_scatter x1, waiting for transfers between devices, reduce_dense(): lax.psum_scatter(grads[3], 'fsdp', scatter_dimension=0, tiled=True)  185 us
    unnamed x2, blocking collectives  160 us
    psum x1, waiting for transfers between devices, on_device(): lax.psum((totals[0], totals[1], totals[2], totals[3], totals[4], totals[5...  120 us
    reduce_scatter x1, waiting for transfers between devices, reduce_dense(): lax.psum_scatter(grads[4], 'fsdp', scatter_dimension=0, tiled=True)  116 us
    reduce_scatter x1, waiting for transfers between devices, reduce_dense(): lax.psum_scatter(grads[6], 'fsdp', scatter_dimension=0, tiled=True)  89.2 us
    all_gather x1, waiting for transfers between devices, fetch_dense(): lax.all_gather(w_query, 'fsdp', axis=0, tiled=True)  69.3 us
  transfers between devices with their start and end apart: 19, of which 17 were waited for; matrix products, arithmetic and copies ran while one was open for 10% of the time, Pallas kernels for 0%

profile of v1, /device:TPU:1, one launch (start us, length us, event | category | flops | bytes accessed | tf_op | source)
XLA Modules:
  0.0 1867.2 jit_solution(7884235925207431253)
XLA Ops:
  11.0 11.3 all-to-all-start
  29.1 82.1 %all-reduce.7 = (bf16[1024]{0:T(1024)(128)(2,1)S(1)}, bf16[1024]{0:T(1024)(128)(2,1)S(1)}) all-reduce(bf16[1024]{0:T(1024)(128)(2,1)S(1)} %dynamic-update-slice, bf16[1024]{0:T(1024)(128)(2,1)S(1)} %dynamic-update-slice.1), channel_id=1, replica_groups=mesh['rep'=4,'fsdp'=32] {'fsdp'}, use_global_device_ids=true, to_apply=%add | all-reduce | flops 2048 | bytes 8192
  126.4 19.1 %all-gather.7.cloned.1.call-done = bf16[1024,512]{1,0:T(8,128)(2,1)} async-done(((bf16[32,512]{1,0:T(8,128)(2,1)}), bf16[1024,512]{1,0:T(8,128)(2,1)}) %all-gather.7.cloned.1.call-update) | async-done | bytes 1048592 | tf_op jit(solution)/shard_map/all_gather | solution.py:127
  147.6 69.3 %all-gather.9.cloned.1.call-done = bf16[1024,1024]{1,0:T(8,128)(2,1)} async-done(((bf16[32,1024]{1,0:T(8,128)(2,1)}), bf16[1024,1024]{1,0:T(8,128)(2,1)}) %all-gather.9.cloned.1.call-update) | async-done | bytes 2097168 | tf_op jit(solution)/shard_map/all_gather | solution.py:126
  225.7 61.9 %all-gather.11.cloned.1.call-done = bf16[1024,1024]{1,0:T(8,128)(2,1)} async-done(((bf16[32,1024]{1,0:T(8,128)(2,1)}), bf16[1024,1024]{1,0:T(8,128)(2,1)}) %all-gather.11.cloned.1.call-update) | async-done | bytes 2097168 | tf_op jit(solution)/shard_map/all_gather | solution.py:129
  319.2 23.5 %all-to-all-done.1 = bf16[32,48,1024]{2,1,0:T(8,128)(2,1)} async-done(((bf16[32,48,1024]{2,1,0:T(8,128)(2,1)}), bf16[32,48,1024]{2,1,0:T(8,128)(2,1)}, u32[]{:S(2)}, u32[]{:S(2)}) %all-to-all-start.1) | async-done | bytes 3145760 | tf_op jit(solution)/shard_map/all_to_all | solution.py:214
  359.5 33.3 %all-to-all-done.5 = bf16[32,48,1024]{2,1,0:T(8,128)(2,1)} async-done(((bf16[32,48,1024]{2,1,0:T(8,128)(2,1)}), bf16[32,48,1024]{2,1,0:T(8,128)(2,1)}, u32[]{:S(2)}, u32[]{:S(2)}) %all-to-all-start.5) | async-done | bytes 3145760 | tf_op jit(solution)/shard_map/all_to_all | solution.py:251
  440.5 17.5 all-to-all-done.2
  458.0 19.6 %all-to-all-start.6 = ((bf16[32,48,1024]{2,1,0:T(8,128)(2,1)}), bf16[32,48,1024]{2,1,0:T(8,128)(2,1)}, u32[]{:S(2)}, u32[]{:S(2)}) async-start(bf16[32,48,1024]{2,1,0:T(8,128)(2,1)} %add_convert_fusion.1), calls=%async_computation.6 | async-start | bytes 6291456 | tf_op jit(solution)/shard_map/all_to_all | solution.py:276
  495.4 22.2 %all-to-all-done.6 = bf16[32,48,1024]{2,1,0:T(8,128)(2,1)} async-done(((bf16[32,48,1024]{2,1,0:T(8,128)(2,1)}), bf16[32,48,1024]{2,1,0:T(8,128)(2,1)}, u32[]{:S(2)}, u32[]{:S(2)}) %all-to-all-start.6) | async-done | bytes 3145760 | tf_op jit(solution)/shard_map/all_to_all | solution.py:276
  537.1 10.6 all-to-all-start.3
  557.2 30.6 %all-to-all-done.3 = bf16[32,48,1024]{2,1,0:T(8,128)(2,1)} async-done(((bf16[32,48,1024]{2,1,0:T(8,128)(2,1)}), bf16[32,48,1024]{2,1,0:T(8,128)(2,1)}, u32[]{:S(2)}, u32[]{:S(2)}) %all-to-all-start.3) | async-done | bytes 3145760 | tf_op jit(solution)/shard_map/all_to_all | solution.py:214
  603.6 35.2 %all-to-all-done.7 = bf16[32,48,1024]{2,1,0:T(8,128)(2,1)} async-done(((bf16[32,48,1024]{2,1,0:T(8,128)(2,1)}), bf16[32,48,1024]{2,1,0:T(8,128)(2,1)}, u32[]{:S(2)}, u32[]{:S(2)}) %all-to-all-start.7) | async-done | bytes 3145760 | tf_op jit(solution)/shard_map/all_to_all | solution.py:251
  653.6 10.6 all-to-all-start.4
  671.2 33.6 %all-to-all-done.4 = bf16[32,48,1024]{2,1,0:T(8,128)(2,1)} async-done(((bf16[32,48,1024]{2,1,0:T(8,128)(2,1)}), bf16[32,48,1024]{2,1,0:T(8,128)(2,1)}, u32[]{:S(2)}, u32[]{:S(2)}) %all-to-all-start.4) | async-done | bytes 3145760 | tf_op jit(solution)/shard_map/all_to_all | solution.py:225
  729.2 26.6 %all-to-all-done.8 = bf16[32,48,1024]{2,1,0:T(8,128)(2,1)S(1)} async-done(((bf16[32,48,1024]{2,1,0:T(8,128)(2,1)}), bf16[32,48,1024]{2,1,0:T(8,128)(2,1)S(1)}, u32[]{:S(2)}, u32[]{:S(2)}) %all-to-all-start.8) | async-done | bytes 3145760 | tf_op jit(solution)/shard_map/all_to_all | solution.py:276
  829.0 116.0 %reduce-scatter.10.cloned.1.call-done = f32[32,512]{1,0:T(8,128)} async-done(((f32[1024,512]{1,0:T(8,128)}), f32[32,512]{1,0:T(8,128)}) %reduce-scatter.10.cloned.1.call-update) | async-done | bytes 65552 | tf_op jit(solution)/shard_map/reduce_scatter | solution.py:142
  945.0 184.9 %reduce-scatter.8.cloned.1.call-done = f32[32,512]{1,0:T(8,128)} async-done(((f32[1024,512]{1,0:T(8,128)}), f32[32,512]{1,0:T(8,128)}) %reduce-scatter.8.cloned.1.call-update) | async-done | bytes 65552 | tf_op jit(solution)/shard_map/reduce_scatter | solution.py:141
  1129.9 191.1 %reduce-scatter.12.cloned.1.call-done = f32[32,1024]{1,0:T(8,128)} async-done(((f32[1024,1024]{1,0:T(8,128)}), f32[32,1024]{1,0:T(8,128)}) %reduce-scatter.12.cloned.1.call-update) | async-done | bytes 131088 | tf_op jit(solution)/shard_map/reduce_scatter | solution.py:143
  1320.9 189.9 %reduce-scatter.6.cloned.1.call-done = f32[32,1024]{1,0:T(8,128)} async-done(((f32[1024,1024]{1,0:T(8,128)}), f32[32,1024]{1,0:T(8,128)}) %reduce-scatter.6.cloned.1.call-update) | async-done | bytes 131088 | tf_op jit(solution)/shard_map/reduce_scatter | solution.py:140
  1519.7 77.4 %all-reduce.4 = (f32[1024]{0:T(1024)S(1)}, f32[1024]{0:T(1024)S(1)}) all-reduce(f32[1024]{0:T(1024)S(1)} %add.332, f32[1024]{0:T(1024)S(1)} %copy-done.96), channel_id=9, replica_groups=mesh['rep'=4,'fsdp'=32] {'fsdp'}, use_global_device_ids=true, to_apply=%region_39.40.clone | all-reduce | flops 2048 | bytes 16384
  1600.5 89.2 %reduce-scatter.14.cloned.1.call-done = f32[32,32]{1,0:T(8,128)} async-done(((f32[1024,32]{1,0:T(8,128)}), f32[32,32]{1,0:T(8,128)}) %reduce-scatter.14.cloned.1.call-update) | async-done | bytes 4112 | tf_op jit(solution)/shard_map/reduce_scatter | solution.py:144
  1689.7 37.0 %all-reduce.5 = (f32[32]{0:T(128)}, f32[32]{0:T(128)}, f32[32,32]{1,0:T(8,128)}) all-reduce(f32[32]{0:T(128)S(1)} %dynamic-slice.3, f32[32]{0:T(128)S(1)} %dynamic-slice.5, f32[32,32]{1,0:T(8,128)} %reduce-scatter.14.cloned.1.call-done), channel_id=1, replica_groups=mesh['rep'=4,'fsdp'=32] {'rep'}, use_global_device_ids=true, to_apply=%region_42.43 | all-reduce | flops 1088 | bytes 8704 | tf_op jit(solution)/shard_map/psum | solution.py:342
  1726.7 120.2 %all-reduce.10.cloned.1.call-done = (f32[32,1024]{1,0:T(8,128)}, f32[32,512]{1,0:T(8,128)}, f32[32,512]{1,0:T(8,128)}, f32[32,1024]{1,0:T(8,128)}, f32[1,1024,51...) async-done(((f32[32,1024]{1,0:T(8,128)}, f32[32,512]{1,0:T(8,128)}, f32[32,512]{1,0:T(8,128)}, f32[32,1024]{1,0:T(8,128)}, f32[1,1024,512]{2,1,0:T(8,128)}, ...) | async-done | bytes 6684688 | tf_op jit(solution)/shard_map/psum | solution.py:342
  (479 shorter events, 336.5 us)
Async XLA Ops:
  7.2 389.9 %copy-start = (bf16[1,1024,512]{2,1,0:T(8,128)(2,1)S(1)}, bf16[1,1024,512]{2,1,0:T(8,128)(2,1)}, u32[]{:S(2)}) copy-start(bf16[1,1024,512]{2,1,0:T(8,128)(2,1)} %param.25) | copy-start | bytes 3145732
  7.2 116.2 %copy-start.103 = (s32[2,1,128]{2,1,0:T(1,128)S(1)}, s32[2,1,128]{2,1,0:T(1,128)}, u32[]{:S(2)}) copy-start(s32[2,1,128]{2,1,0:T(1,128)} %param.15) | copy-start | bytes 3076
  7.2 116.0 %copy-start.2 = (bf16[2,1,128,1024]{3,2,1,0:T(8,128)(2,1)S(1)}, bf16[2,1,128,1024]{3,2,1,0:T(8,128)(2,1)}, u32[]{:S(2)}) copy-start(bf16[2,1,128,1024]{3,2,1,0:T(8,128)(2,1)} %param.14) | copy-start | bytes 1572868
  7.2 117.5 %all-gather.5.cloned.1.call-start = ((), (), s32[]{:S(2)}) async-start(), calls=%async_computation.14 | async-start | bytes 1081344 | tf_op jit(solution)/shard_map/all_gather | solution.py:128
  8.0 137.5 %all-gather.7.cloned.1.call-start = ((), (), s32[]{:S(2)}) async-start(), calls=%async_computation.15 | async-start | bytes 1081344 | tf_op jit(solution)/shard_map/all_gather | solution.py:127
  8.7 208.2 %all-gather.9.cloned.1.call-start = ((), (), s32[]{:S(2)}) async-start(), calls=%async_computation.16 | async-start | bytes 2162688 | tf_op jit(solution)/shard_map/all_gather | solution.py:126
  11.0 287.0 %all-to-all-start = ((bf16[32,2,512]{2,1,0:T(2,128)(2,1)}), bf16[32,2,512]{2,1,0:T(2,128)(2,1)S(1)}, u32[]{:S(2)}, u32[]{:S(2)}) async-start(bf16[32,2,512]{2,1,0:T(2,128)(2,1)} %reshape.1095), calls=%async_computation | async-start | bytes 131072 | tf_op jit(solution)/shard_map/all_to_all | solution.py:131
  22.4 265.2 %all-gather.11.cloned.1.call-start = ((), (), s32[]{:S(2)}) async-start(), calls=%async_computation.17 | async-start | bytes 2162688 | tf_op jit(solution)/shard_map/all_gather | solution.py:129
  113.7 109.5 %copy-start.68 = (f32[128,64]{0,1:T(8,128)}, f32[128,64]{0,1:T(8,128)S(1)}, u32[]{:S(2)}) copy-start(f32[128,64]{0,1:T(8,128)S(1)} %get-tuple-element.115) | copy-start | bytes 98308
  124.0 166.7 %copy-start.94 = (s32[1024,1]{0,1:T(1,128)}, s32[1024,1]{0,1:T(1,128)S(1)}, u32[]{:S(2)}) copy-start(s32[1024,1]{0,1:T(1,128)S(1)} %compare_select_fusion.1) | copy-start | bytes 12292
  298.0 44.7 %all-to-all-start.1 = ((bf16[32,48,1024]{2,1,0:T(8,128)(2,1)}), bf16[32,48,1024]{2,1,0:T(8,128)(2,1)}, u32[]{:S(2)}, u32[]{:S(2)}) async-start(bf16[32,48,1024]{2,1,0:T(8,128)(2,1)} %bitcast.623), calls=%async_computation.1 | async-start | bytes 6291456 | tf_op jit(solution)/shard_map/all_to_all | solution.py:214
  342.7 50.1 %all-to-all-start.5 = ((bf16[32,48,1024]{2,1,0:T(8,128)(2,1)}), bf16[32,48,1024]{2,1,0:T(8,128)(2,1)}, u32[]{:S(2)}, u32[]{:S(2)}) async-start(bf16[32,48,1024]{2,1,0:T(8,128)(2,1)} %bitcast.625), calls=%async_computation.5 | async-start | bytes 6291456 | tf_op jit(solution)/shard_map/all_to_all | solution.py:251
  408.2 49.8 %all-to-all-start.2 = ((bf16[32,48,1024]{2,1,0:T(8,128)(2,1)}), bf16[32,48,1024]{2,1,0:T(8,128)(2,1)}, u32[]{:S(2)}, u32[]{:S(2)}) async-start(bf16[32,48,1024]{2,1,0:T(8,128)(2,1)} %convolution_convert_fusion.1), calls=%async_computation.2 | async-start | bytes 6291456 | tf_op jit(solution)/shard_map/all_to_all | solution.py:225
  458.0 59.6 %all-to-all-start.6 = ((bf16[32,48,1024]{2,1,0:T(8,128)(2,1)}), bf16[32,48,1024]{2,1,0:T(8,128)(2,1)}, u32[]{:S(2)}, u32[]{:S(2)}) async-start(bf16[32,48,1024]{2,1,0:T(8,128)(2,1)} %add_convert_fusion.1), calls=%async_computation.6 | async-start | bytes 6291456 | tf_op jit(solution)/shard_map/all_to_all | solution.py:276
  537.1 50.7 %all-to-all-start.3 = ((bf16[32,48,1024]{2,1,0:T(8,128)(2,1)}), bf16[32,48,1024]{2,1,0:T(8,128)(2,1)}, u32[]{:S(2)}, u32[]{:S(2)}) async-start(bf16[32,48,1024]{2,1,0:T(8,128)(2,1)} %bitcast.624), calls=%async_computation.3 | async-start | bytes 6291456 | tf_op jit(solution)/shard_map/all_to_all | solution.py:214
  587.8 50.9 %all-to-all-start.7 = ((bf16[32,48,1024]{2,1,0:T(8,128)(2,1)}), bf16[32,48,1024]{2,1,0:T(8,128)(2,1)}, u32[]{:S(2)}, u32[]{:S(2)}) async-start(bf16[32,48,1024]{2,1,0:T(8,128)(2,1)} %bitcast.626), calls=%async_computation.7 | async-start | bytes 6291456 | tf_op jit(solution)/shard_map/all_to_all | solution.py:251
  653.6 51.2 %all-to-all-start.4 = ((bf16[32,48,1024]{2,1,0:T(8,128)(2,1)}), bf16[32,48,1024]{2,1,0:T(8,128)(2,1)}, u32[]{:S(2)}, u32[]{:S(2)}) async-start(bf16[32,48,1024]{2,1,0:T(8,128)(2,1)} %convolution_convert_fusion), calls=%async_computation.4 | async-start | bytes 6291456 | tf_op jit(solution)/shard_map/all_to_all | solution.py:225
  704.8 51.0 %all-to-all-start.8 = ((bf16[32,48,1024]{2,1,0:T(8,128)(2,1)}), bf16[32,48,1024]{2,1,0:T(8,128)(2,1)S(1)}, u32[]{:S(2)}, u32[]{:S(2)}) async-start(bf16[32,48,1024]{2,1,0:T(8,128)(2,1)} %add_convert_fusion), calls=%async_computation.8 | async-start | bytes 6291456 | tf_op jit(solution)/shard_map/all_to_all | solution.py:276
  715.3 229.7 %reduce-scatter.10.cloned.1.call-start = ((), (), s32[]{:S(2)}) async-start(), calls=%async_computation.20 | async-start | bytes 2162688 | tf_op jit(solution)/shard_map/reduce_scatter | solution.py:142
  779.7 350.2 %reduce-scatter.8.cloned.1.call-start = ((), (), s32[]{:S(2)}) async-start(), calls=%async_computation.19 | async-start | bytes 2162688 | tf_op jit(solution)/shard_map/reduce_scatter | solution.py:141
  786.3 534.7 %reduce-scatter.12.cloned.1.call-start = ((), (), s32[]{:S(2)}) async-start(), calls=%async_computation.21 | async-start | bytes 4325376 | tf_op jit(solution)/shard_map/reduce_scatter | solution.py:143
  790.1 720.8 %reduce-scatter.6.cloned.1.call-start = ((), (), s32[]{:S(2)}) async-start(), calls=%async_computation.18 | async-start | bytes 4325376 | tf_op jit(solution)/shard_map/reduce_scatter | solution.py:140
  797.5 892.2 %reduce-scatter.14.cloned.1.call-start = ((), (), s32[]{:S(2)}) async-start(), calls=%async_computation.22 | async-start | bytes 540672 | tf_op jit(solution)/shard_map/reduce_scatter | solution.py:144
  822.5 1024.4 %all-reduce.10.cloned.1.call-start = ((), (), s32[]{:S(2)}) async-start(), calls=%async_computation.23 | async-start | bytes 13369344 | tf_op jit(solution)/shard_map/psum | solution.py:342
  (118 other events, 1567.2 us)
Sparse Core Ops, SparseCore 0:
  11.0 67.9 all-gather.4
  82.0 63.4 all-gather.6
  148.6 68.2 all-gather.8
  219.8 67.6 all-gather.10
  779.8 165.1 reduce-scatter.9
  947.9 181.9 reduce-scatter.7
  1132.3 188.6 reduce-scatter.11
  1323.3 187.4 reduce-scatter.5
  1513.2 176.4 reduce-scatter.13
  1693.5 153.3 all-reduce.9
